TPU v7x, 128 devices: a whole 4x4x4 slice. The times are simulated.
128 devices in a mesh: cube: 32 (over x, z, y_hi), grid: 4 (over y_lo, core).
Axes of the slice: x: 4, y: 4 (y_hi: 2, y_lo: 2; y = y_hi * 2 + y_lo), z: 4, core: 2. Of those that a mesh axis runs over, the one named last changes fastest.
Arguments:
- front_root: float32 [16384, 16384], P('cube', 'grid'), as said below
- front_upper: float32 [16384, 8192], P('cube', 'grid'), as said below
- front_middle: float32 [16384, 4096], P('cube', 'grid'), as said below
- front_lower: float32 [16384, 2048], P('cube', 'grid'), as said below
- place_upper: int32 [2, 62], replicated, may hold values from 0 to 127, as said below
- place_middle: int32 [4, 30], replicated, may hold values from 0 to 63, as said below
- place_lower: int32 [8, 14], replicated, may hold values from 0 to 31, as said below
Outputs:
- factor_root: float32 [16384, 256], P('cube')
- factor_upper: float32 [16384, 256], P('cube')
- factor_middle: float32 [16384, 256], P('cube')
- factor_lower: float32 [16384, 256], P('cube')
- root_rest: float32 [16384, 16384], P('cube', 'grid')
Inputs may be any that keep to these rules, and one draw needn't show every extreme that they name: `front_root`: each front is symmetric positive definite, with diagonal entries of at least 2 and all entries of magnitude at most 12. `front_upper`: each front is symmetric positive definite, with diagonal entries of at least 2 and all entries of magnitude at most 12. `front_middle`: each front is symmetric positive definite, with diagonal entries of at least 2 and all entries of magnitude at most 12. `front_lower`: each front is symmetric positive definite, with diagonal entries of at least 2 and all entries of magnitude at most 12. `place_upper`: row c lists the parent block row of child c's block row 2 + u; within a row the values are distinct, and each is congruent to 2 + u modulo max(16, G). `place_middle`: row c lists the parent block row of child c's block row 2 + u; within a row the values are distinct, and each is congruent to 2 + u modulo max(8, G). `place_lower`: row c lists the parent block row of child c's block row 2 + u; within a row the values are distinct, and each is congruent to 2 + u modulo max(4, G).
All inputs are finite; a program needn't handle non-finite values.
Results may differ from a plain program's by a relative error of at most 0.0001.
Values sent between devices are 32-bit elements; how exact they have to be, the bound alone decides.
No kernel may reach another device: no remote copies, remote signals or barrier semaphores. Data moves between devices by JAX's collectives and lax.ppermute only.
A program may use at most 192 MiB of HBM per device.

v0:
```python
import jax
import jax.numpy as jnp
from jax import lax
from jax.sharding import PartitionSpec as P

BS = 128
PIVOTS = 2
ROWS = 4


HIGHEST = lax.Precision.HIGHEST


def swapped(block, axis, stride):
    count = lax.axis_size(axis)
    route = []
    for low in range(count):
        high = low | 1 << stride
        if high != low and high < count:
            route += [(low, high), (high, low)]
    return lax.ppermute(block, axis, route)


def broadcast(array, axis, root):
    mine = lax.axis_index(axis) == root
    return lax.psum(jnp.where(mine, array, jnp.zeros_like(array)), axis)


def inverse_lower(lower_tri):
    ident = jnp.eye(lower_tri.shape[0], dtype=jnp.float32)
    return jax.scipy.linalg.solve_triangular(lower_tri, ident, lower=True)


def along_cube(panel_piece, sub_size, cube_at):
    collected = panel_piece[None]
    for which_bit in range(sub_size.bit_length() - 1):
        partner = swapped(collected, "cube", which_bit)
        high_half = cube_at >> which_bit & 1 == 1
        collected = jnp.where(
            high_half,
            jnp.concatenate([partner, collected], 0),
            jnp.concatenate([collected, partner], 0),
        )
    return collected


def whole_column(panel_piece, sub_size, cube_at, owner_grid):
    shared = broadcast(panel_piece, "grid", owner_grid)
    return along_cube(shared, sub_size, cube_at)


def full_columns(panel_piece, pivot_at, sub_size, grid_count, cube_at, my_slot, col_ids, all_ids):
    column = whole_column(panel_piece, sub_size, cube_at, pivot_at % grid_count)
    blocks = column.reshape(sub_size, ROWS, BS, BS)
    lower_tri = jnp.linalg.cholesky(blocks[pivot_at % sub_size, pivot_at // sub_size])
    inverse_t = inverse_lower(lower_tri).T
    solved = jnp.dot(column.reshape(sub_size * ROWS * BS, BS), inverse_t, precision=HIGHEST)
    solved = solved.reshape(sub_size, ROWS, BS, BS)
    solved = jnp.where((all_ids > pivot_at)[:, :, None, None], solved, jnp.float32(0.0))
    solved = jnp.where((all_ids == pivot_at)[:, :, None, None], lower_tri[None, None], solved)
    own_rows = lax.dynamic_index_in_dim(solved, my_slot, 0, keepdims=False)
    col_blocks = solved[col_ids % sub_size, col_ids // sub_size]
    return (own_rows, col_blocks)


def eliminate_front(front_tile, depth_level, cube_count, grid_count, cube_at, grid_at):
    sub_size = cube_count >> depth_level
    my_slot = cube_at % sub_size
    block_order = ROWS * sub_size
    local_cols = block_order // grid_count
    row_ids = jnp.arange(ROWS) * sub_size + my_slot
    col_ids = jnp.arange(local_cols) * grid_count + grid_at
    all_ids = jnp.arange(ROWS)[None, :] * sub_size + jnp.arange(sub_size)[:, None]
    factors = []
    for pivot_at in range(PIVOTS):
        col_start = pivot_at // grid_count * BS
        panel_piece = front_tile[:, col_start : col_start + BS]
        own_rows, col_blocks = full_columns(
            panel_piece, pivot_at, sub_size, grid_count, cube_at, my_slot, col_ids, all_ids
        )
        row_terms = jnp.where(
            (row_ids > pivot_at)[:, None, None], own_rows, jnp.float32(0.0)
        ).reshape(ROWS * BS, BS)
        col_terms = jnp.where(
            (col_ids > pivot_at)[:, None, None], col_blocks, jnp.float32(0.0)
        ).reshape(local_cols * BS, BS)
        front_tile = front_tile - jnp.dot(row_terms, col_terms.T, precision=HIGHEST)
        factors.append(own_rows.reshape(ROWS * BS, BS))
    return (front_tile, jnp.concatenate(factors, 1))


def place_update(front_tile, mapping, child_size, child_slot, target_slot, grid_count, grid_at):
    parent_size = 2 * child_size
    child_cols = front_tile.shape[1] // BS
    parent_cols = 2 * child_cols
    row_ids = jnp.arange(ROWS) * child_size + child_slot
    col_ids = jnp.arange(child_cols) * grid_count + grid_at
    row_dest = mapping[jnp.maximum(row_ids - PIVOTS, 0)]
    col_dest = mapping[jnp.maximum(col_ids - PIVOTS, 0)]
    row_valid = (row_ids >= PIVOTS) & (row_dest % parent_size == target_slot)
    row_pick = row_valid[None, :] & (
        (row_dest // parent_size)[None, :] == jnp.arange(ROWS)[:, None]
    )
    col_pick = (col_ids >= PIVOTS)[None, :] & (
        (col_dest // grid_count)[None, :] == jnp.arange(parent_cols)[:, None]
    )
    row_source = jnp.sum(jnp.where(row_pick, jnp.arange(ROWS)[None, :], 0), 1)
    row_present = jnp.any(row_pick, 1)
    col_source = jnp.sum(jnp.where(col_pick, jnp.arange(child_cols)[None, :], 0), 1)
    col_present = jnp.any(col_pick, 1)
    blocks = front_tile.reshape(ROWS, BS, child_cols, BS)
    taken = jnp.take(jnp.take(blocks, row_source, axis=0), col_source, axis=2)
    keep_mask = row_present[:, None, None, None] & col_present[None, None, :, None]
    placed = jnp.where(keep_mask, taken, jnp.float32(0.0))
    return placed.reshape(ROWS * BS, parent_cols * BS)


def extend_parent(
    parent_tile, child_tile, table, child_depth, cube_count, grid_count, cube_at, grid_at
):
    child_size = cube_count >> child_depth
    parent_slot = cube_at % (2 * child_size)
    child_slot = cube_at % child_size
    child_front = cube_at // child_size
    which_bit = child_size.bit_length() - 1
    own_map = lax.dynamic_index_in_dim(table, child_front, 0, keepdims=False)
    kept = place_update(
        child_tile, own_map, child_size, child_slot, parent_slot, grid_count, grid_at
    )
    partner_tile = swapped(child_tile, "cube", which_bit)
    partner_map = lax.dynamic_index_in_dim(table, child_front ^ 1, 0, keepdims=False)
    taken = place_update(
        partner_tile, partner_map, child_size, child_slot, parent_slot, grid_count, grid_at
    )
    return parent_tile + kept + taken


def on_device(
    front_root, front_upper, front_middle, front_lower, place_upper, place_middle, place_lower
):
    cube_count = lax.axis_size("cube")
    grid_count = lax.axis_size("grid")
    cube_at = lax.axis_index("cube")
    grid_at = lax.axis_index("grid")
    stored = (front_root, front_upper, front_middle, front_lower)
    tables = (None, place_upper, place_middle, place_lower)
    factor_list = [None, None, None, None]
    below = None
    for depth_level in (3, 2, 1, 0):
        front_tile = stored[depth_level]
        if below is not None:
            front_tile = extend_parent(
                front_tile,
                below,
                tables[depth_level + 1],
                depth_level + 1,
                cube_count,
                grid_count,
                cube_at,
                grid_at,
            )
        below, factor_list[depth_level] = eliminate_front(
            front_tile, depth_level, cube_count, grid_count, cube_at, grid_at
        )
    local_cols = below.shape[1] // BS
    row_ids = jnp.arange(ROWS) * cube_count + cube_at
    col_ids = jnp.arange(local_cols) * grid_count + grid_at
    keep_mask = (row_ids >= PIVOTS)[:, None, None, None] & (col_ids >= PIVOTS)[None, None, :, None]
    rest = jnp.where(keep_mask, below.reshape(ROWS, BS, local_cols, BS), jnp.float32(0.0)).reshape(
        below.shape
    )
    return (factor_list[0], factor_list[1], factor_list[2], factor_list[3], rest)


def solution(mesh):
    return jax.shard_map(
        on_device,
        mesh=mesh,
        in_specs=(
            P("cube", "grid"),
            P("cube", "grid"),
            P("cube", "grid"),
            P("cube", "grid"),
            P(),
            P(),
            P(),
        ),
        out_specs=(
            P("cube", None),
            P("cube", None),
            P("cube", None),
            P("cube", None),
            P("cube", "grid"),
        ),
        check_vma=False,
    )
```

profile of v0, /device:TPU:30, one launch (start us, length us, event | category | flops | bytes accessed | tf_op | source)
XLA Modules:
  0.0 1644.1 jit_solution(696209560198082043)
XLA Ops:
  13.0 35.5 %all-reduce.9.cloned.1.call-done = f32[512,128]{1,0:T(8,128)} async-done(((f32[512,128]{1,0:T(8,128)}), f32[512,128]{1,0:T(8,128)}) %all-reduce.9.cloned.1.call-update) | async-done | bytes 262160 | tf_op jit(solution)/shard_map/psum | solution.py:26
  49.7 9.1 collective-permute-done
  62.8 10.5 collective-permute-done.1
  73.6 11.7 cholesky.134
  86.7 9.8 custom-call.28
  101.1 37.2 %all-reduce.11.cloned.1.call-done = f32[512,128]{1,0:T(8,128)} async-done(((f32[512,128]{1,0:T(8,128)}), f32[512,128]{1,0:T(8,128)}) %all-reduce.11.cloned.1.call-update) | async-done | bytes 262160 | tf_op jit(solution)/shard_map/psum | solution.py:26
  139.7 8.9 collective-permute-done.2
  152.9 10.4 collective-permute-done.3
  163.6 11.7 cholesky.145
  176.7 9.8 custom-call.29
  200.4 16.3 collective-permute-done.4
  225.6 37.0 %all-reduce.13.cloned.1.call-done = f32[512,128]{1,0:T(8,128)} async-done(((f32[512,128]{1,0:T(8,128)}), f32[512,128]{1,0:T(8,128)}) %all-reduce.13.cloned.1.call-update) | async-done | bytes 262160 | tf_op jit(solution)/shard_map/psum | solution.py:26
  265.1 7.8 collective-permute-done.5
  275.6 11.8 collective-permute-done.6
  295.1 18.1 %collective-permute-done.7 = f32[4,512,128]{2,1,0:T(8,128)S(1)} collective-permute-done((f32[4,512,128]{2,1,0:T(8,128)S(1)}, f32[4,512,128]{2,1,0:T(8,128)S(1)}, u32[]{:S(2)}, u32[]{:S(2)}) %collective-permute-start.7) | collective-permute-done | bytes 1048608 | tf_op jit(solution)/shard_map/ppermute | solution.py:21
  315.4 11.7 cholesky.156
  328.5 9.8 custom-call.30
  346.3 37.3 %all-reduce.15.cloned.1.call-done = f32[512,128]{1,0:T(8,128)} async-done(((f32[512,128]{1,0:T(8,128)}), f32[512,128]{1,0:T(8,128)}) %all-reduce.15.cloned.1.call-update) | async-done | bytes 262160 | tf_op jit(solution)/shard_map/psum | solution.py:26
  386.1 7.8 collective-permute-done.8
  396.8 11.7 collective-permute-done.9
  421.3 13.6 collective-permute-done.10
  438.5 11.7 cholesky.167
  451.6 9.8 custom-call.31
  491.6 28.2 %collective-permute-done.11 = f32[512,1024]{1,0:T(8,128)} collective-permute-done((f32[512,1024]{1,0:T(8,128)}, f32[512,1024]{1,0:T(8,128)}, u32[]{:S(2)}, u32[]{:S(2)}) %collective-permute-start.11) | collective-permute-done | bytes 2097184 | tf_op jit(solution)/shard_map/ppermute | solution.py:21
  542.2 37.1 %all-reduce.17.cloned.1.call-done = f32[512,128]{1,0:T(8,128)} async-done(((f32[512,128]{1,0:T(8,128)}), f32[512,128]{1,0:T(8,128)}) %all-reduce.17.cloned.1.call-update) | async-done | bytes 262160 | tf_op jit(solution)/shard_map/psum | solution.py:26
  580.4 9.1 collective-permute-done.12
  592.2 11.8 collective-permute-done.13
  607.4 22.0 %collective-permute-done.14 = f32[4,512,128]{2,1,0:T(8,128)S(1)} collective-permute-done((f32[4,512,128]{2,1,0:T(8,128)S(1)}, f32[4,512,128]{2,1,0:T(8,128)S(1)}, u32[]{:S(2)}, u32[]{:S(2)}) %collective-permute-start.14) | collective-permute-done | bytes 1048608 | tf_op jit(solution)/shard_map/ppermute | solution.py:21
  637.5 39.0 %collective-permute-done.15 = f32[8,512,128]{2,1,0:T(8,128)} collective-permute-done((f32[8,512,128]{2,1,0:T(8,128)}, f32[8,512,128]{2,1,0:T(8,128)}, u32[]{:S(2)}, u32[]{:S(2)}) %collective-permute-start.15) | collective-permute-done | bytes 2097184 | tf_op jit(solution)/shard_map/ppermute | solution.py:21
  680.5 11.7 cholesky.178
  693.6 9.8 custom-call.32
  724.9 37.1 %all-reduce.19.cloned.1.call-done = f32[512,128]{1,0:T(8,128)} async-done(((f32[512,128]{1,0:T(8,128)}), f32[512,128]{1,0:T(8,128)}) %all-reduce.19.cloned.1.call-update) | async-done | bytes 262160 | tf_op jit(solution)/shard_map/psum | solution.py:26
  763.2 9.1 collective-permute-done.16
  775.0 11.8 collective-permute-done.17
  790.5 22.0 %collective-permute-done.18 = f32[4,512,128]{2,1,0:T(8,128)S(1)} collective-permute-done((f32[4,512,128]{2,1,0:T(8,128)S(1)}, f32[4,512,128]{2,1,0:T(8,128)S(1)}, u32[]{:S(2)}, u32[]{:S(2)}) %collective-permute-start.18) | collective-permute-done | bytes 1048608 | tf_op jit(solution)/shard_map/ppermute | solution.py:21
  821.4 38.3 %collective-permute-done.19 = f32[8,512,128]{2,1,0:T(8,128)} collective-permute-done((f32[8,512,128]{2,1,0:T(8,128)}, f32[8,512,128]{2,1,0:T(8,128)}, u32[]{:S(2)}, u32[]{:S(2)}) %collective-permute-start.19) | collective-permute-done | bytes 2097184 | tf_op jit(solution)/shard_map/ppermute | solution.py:21
  863.5 11.7 cholesky.189
  876.6 9.8 custom-call.33
  925.1 6.7 gather_fusion.29
  935.7 8.1 copy.253
  943.8 54.2 %collective-permute-done.20 = f32[512,2048]{1,0:T(8,128)} collective-permute-done((f32[512,2048]{1,0:T(8,128)}, f32[512,2048]{1,0:T(8,128)}, u32[]{:S(2)}, u32[]{:S(2)}) %collective-permute-start.20) | collective-permute-done | bytes 4194336 | tf_op jit(solution)/shard_map/ppermute | solution.py:21
  1014.0 6.7 gather_fusion.31
  1029.9 20.9 %bitcast_add_fusion = f32[512,4096]{1,0:T(8,128)S(1)} fusion(f32[64,8,32,128]{3,2,1,0:T(8,128)S(1)} %bitcast.321, f32[512,4096]{1,0:T(8,128)} %param.22, f32[64,8,32,128]{3,2,1,0:T(8,128)} %bitcast.320), kind=kLoop, calls=%fused_computation.32 | loop fusion | flops 4194304 | bytes 33554432 | tf_op jit(solution)/shard_map/add | solution.py:135
  1055.1 37.1 %all-reduce.21.cloned.1.call-done = f32[1,512,128]{2,1,0:T(8,128)} async-done(((f32[1,512,128]{2,1,0:T(8,128)}), f32[1,512,128]{2,1,0:T(8,128)}) %all-reduce.21.cloned.1.call-update) | async-done | bytes 262160 | tf_op jit(solution)/shard_map/psum | solution.py:26
  1093.3 9.1 collective-permute-done.21
  1105.1 11.8 collective-permute-done.22
  1120.2 22.0 %collective-permute-done.23 = f32[4,512,128]{2,1,0:T(8,128)S(1)} collective-permute-done((f32[4,512,128]{2,1,0:T(8,128)S(1)}, f32[4,512,128]{2,1,0:T(8,128)S(1)}, u32[]{:S(2)}, u32[]{:S(2)}) %collective-permute-start.23) | collective-permute-done | bytes 1048608 | tf_op jit(solution)/shard_map/ppermute | solution.py:21
  1144.2 44.4 %collective-permute-done.24 = f32[8,512,128]{2,1,0:T(8,128)S(1)} collective-permute-done((f32[8,512,128]{2,1,0:T(8,128)S(1)}, f32[8,512,128]{2,1,0:T(8,128)S(1)}, u32[]{:S(2)}, u32[]{:S(2)}) %collective-permute-start.24) | collective-permute-done | bytes 2097184 | tf_op jit(solution)/shard_map/ppermute | solution.py:21
  1210.2 71.8 %collective-permute-done.25 = f32[16,512,128]{2,1,0:T(8,128)} collective-permute-done((f32[16,512,128]{2,1,0:T(8,128)}, f32[16,512,128]{2,1,0:T(8,128)}, u32[]{:S(2)}, u32[]{:S(2)}) %collective-permute-start.25) | collective-permute-done | bytes 4194336 | tf_op jit(solution)/shard_map/ppermute | solution.py:21
  1288.4 11.7 cholesky.200
  1301.4 9.8 custom-call.34
  1317.9 9.0 select_select_fusion.1
  1332.9 9.3 convolution_subtract_fusion
  1346.2 37.2 %all-reduce.23.cloned.1.call-done = f32[1,512,128]{2,1,0:T(8,128)} async-done(((f32[1,512,128]{2,1,0:T(8,128)}), f32[1,512,128]{2,1,0:T(8,128)}) %all-reduce.23.cloned.1.call-update) | async-done | bytes 262160 | tf_op jit(solution)/shard_map/psum | solution.py:26
  1384.5 9.1 collective-permute-done.26
  1396.3 11.8 collective-permute-done.27
  1411.4 22.0 %collective-permute-done.28 = f32[4,512,128]{2,1,0:T(8,128)S(1)} collective-permute-done((f32[4,512,128]{2,1,0:T(8,128)S(1)}, f32[4,512,128]{2,1,0:T(8,128)S(1)}, u32[]{:S(2)}, u32[]{:S(2)}) %collective-permute-start.28) | collective-permute-done | bytes 1048608 | tf_op jit(solution)/shard_map/ppermute | solution.py:21
  1435.4 44.4 %collective-permute-done.29 = f32[8,512,128]{2,1,0:T(8,128)S(1)} collective-permute-done((f32[8,512,128]{2,1,0:T(8,128)S(1)}, f32[8,512,128]{2,1,0:T(8,128)S(1)}, u32[]{:S(2)}, u32[]{:S(2)}) %collective-permute-start.29) | collective-permute-done | bytes 2097184 | tf_op jit(solution)/shard_map/ppermute | solution.py:21
  1497.8 6.6 maximum_select_fusion.7
  1504.3 68.9 %collective-permute-done.30 = f32[16,512,128]{2,1,0:T(8,128)} collective-permute-done((f32[16,512,128]{2,1,0:T(8,128)}, f32[16,512,128]{2,1,0:T(8,128)}, u32[]{:S(2)}, u32[]{:S(2)}) %collective-permute-start.30) | collective-permute-done | bytes 4194336 | tf_op jit(solution)/shard_map/ppermute | solution.py:21
  1579.6 11.7 cholesky.211
  1592.7 9.8 custom-call.35
  1609.2 9.0 select_select_fusion
  1625.1 12.0 subtract_select_fusion
  (448 shorter events, 385.4 us)
Async XLA Ops:
  7.2 41.3 %all-reduce.9.cloned.1.call-start = ((), (), s32[]{:S(2)}) async-start(), calls=%async_computation | async-start | bytes 524288 | tf_op jit(solution)/shard_map/psum | solution.py:26
  8.9 129.4 %all-reduce.11.cloned.1.call-start = ((), (), s32[]{:S(2)}) async-start(), calls=%async_computation.1 | async-start | bytes 524288 | tf_op jit(solution)/shard_map/psum | solution.py:26
  48.5 10.3 collective-permute-start
  59.8 13.4 collective-permute-start.1
  73.5 25.8 %copy-start.12 = (f32[512,512]{1,0:T(8,128)S(1)}, f32[512,512]{1,0:T(8,128)}, u32[]{:S(2)}) copy-start(f32[512,512]{1,0:T(8,128)} %param.25) | copy-start | bytes 3145732
  101.0 161.6 %all-reduce.13.cloned.1.call-start = ((), (), s32[]{:S(2)}) async-start(), calls=%async_computation.2 | async-start | bytes 524288 | tf_op jit(solution)/shard_map/psum | solution.py:26
  138.3 10.3 collective-permute-start.2
  149.7 13.6 collective-permute-start.3
  191.2 25.5 %collective-permute-start.4 = (f32[512,512]{1,0:T(8,128)}, f32[512,512]{1,0:T(8,128)}, u32[]{:S(2)}, u32[]{:S(2)}) collective-permute-start(f32[512,512]{1,0:T(8,128)} %convolution_subtract_fusion.5), channel_id=1, source_target_pairs={{0,16},{16,0},{4,20},{20,4},{8,24},{24,8},{12,28},{28,12},{32,48},... | collective-permute-start | bytes 3145736 | tf_op jit(solution)/shard_map/ppermute | solution.py:21
  219.9 1.6 copy-start.6
  219.9 2.2 copy-start.11
  222.1 3.4 copy-start.25
  223.4 1.3 copy-start.5
  225.5 158.1 %all-reduce.15.cloned.1.call-start = ((), (), s32[]{:S(2)}) async-start(), calls=%async_computation.3 | async-start | bytes 524288 | tf_op jit(solution)/shard_map/psum | solution.py:26
  262.6 28.7 %copy-start.19 = (f32[512,128]{1,0:T(8,128)S(1)}, f32[512,128]{1,0:T(8,128)}, u32[]{:S(2)}) copy-start(f32[512,128]{1,0:T(8,128)} %all-reduce.13.cloned.1.call-done) | copy-start | bytes 786436
  262.6 10.3 collective-permute-start.5
  274.0 13.4 collective-permute-start.6
  287.5 25.7 %collective-permute-start.7 = (f32[4,512,128]{2,1,0:T(8,128)S(1)}, f32[4,512,128]{2,1,0:T(8,128)S(1)}, u32[]{:S(2)}, u32[]{:S(2)}) collective-permute-start(f32[4,512,128]{2,1,0:T(8,128)S(1)} %maximum_select_fusion.20), channel_id=1, source_target_pairs={{0,16},{16,0},{4,20},{20,4},{8,24},{24,8},{12,28},{28,12},{32,48},... | collective-permute-start | bytes 3145736 | tf_op jit(solution)/shard_map/ppermute | solution.py:21
  346.3 233.0 %all-reduce.17.cloned.1.call-start = ((), (), s32[]{:S(2)}) async-start(), calls=%async_computation.4 | async-start | bytes 524288 | tf_op jit(solution)/shard_map/psum | solution.py:26
  383.6 29.2 %copy-start.22 = (f32[512,128]{1,0:T(8,128)S(1)}, f32[512,128]{1,0:T(8,128)}, u32[]{:S(2)}) copy-start(f32[512,128]{1,0:T(8,128)} %all-reduce.15.cloned.1.call-done) | copy-start | bytes 786436
  383.6 10.3 collective-permute-start.8
  393.9 2.9 copy-start.23
  395.1 13.4 collective-permute-start.9
  409.4 25.5 %collective-permute-start.10 = (f32[4,512,128]{2,1,0:T(8,128)S(1)}, f32[4,512,128]{2,1,0:T(8,128)}, u32[]{:S(2)}, u32[]{:S(2)}) collective-permute-start(f32[4,512,128]{2,1,0:T(8,128)S(1)} %maximum_select_fusion.22), channel_id=1, source_target_pairs={{0,16},{16,0},{4,20},{20,4},{8,24},{24,8},{12,28},{28,12},{32,48},... | collective-permute-start | bytes 3145736 | tf_op jit(solution)/shard_map/ppermute | solution.py:21
  473.8 45.9 %collective-permute-start.11 = (f32[512,1024]{1,0:T(8,128)}, f32[512,1024]{1,0:T(8,128)}, u32[]{:S(2)}, u32[]{:S(2)}) collective-permute-start(f32[512,1024]{1,0:T(8,128)} %convolution_subtract_fusion.3), channel_id=1, source_target_pairs={{0,32},{32,0},{4,36},{36,4},{8,40},{40,8},{12,44},{44,12},{16,48},... | collective-permute-start | bytes 6291464 | tf_op jit(solution)/shard_map/ppermute | solution.py:21
  531.5 2.5 copy-start.4
  531.5 3.5 copy-start.9
  539.4 2.0 copy-start.3
  542.1 219.9 %all-reduce.19.cloned.1.call-start = ((), (), s32[]{:S(2)}) async-start(), calls=%async_computation.5 | async-start | bytes 524288 | tf_op jit(solution)/shard_map/psum | solution.py:26
  579.3 52.6 %copy-start.21 = (f32[512,128]{1,0:T(8,128)S(1)}, f32[512,128]{1,0:T(8,128)}, u32[]{:S(2)}) copy-start(f32[512,128]{1,0:T(8,128)} %all-reduce.17.cloned.1.call-done) | copy-start | bytes 786436
  579.3 10.3 collective-permute-start.12
  590.6 13.4 collective-permute-start.13
  604.1 25.3 %collective-permute-start.14 = (f32[4,512,128]{2,1,0:T(8,128)S(1)}, f32[4,512,128]{2,1,0:T(8,128)S(1)}, u32[]{:S(2)}, u32[]{:S(2)}) collective-permute-start(f32[4,512,128]{2,1,0:T(8,128)S(1)} %maximum_select_fusion.24), channel_id=1, source_target_pairs={{0,16},{16,0},{4,20},{20,4},{8,24},{24,8},{12,28},{28,12},{32,48},... | collective-permute-start | bytes 3145736 | tf_op jit(solution)/shard_map/ppermute | solution.py:21
  630.9 45.5 %collective-permute-start.15 = (f32[8,512,128]{2,1,0:T(8,128)}, f32[8,512,128]{2,1,0:T(8,128)}, u32[]{:S(2)}, u32[]{:S(2)}) collective-permute-start(f32[8,512,128]{2,1,0:T(8,128)} %maximum_select_fusion.10), channel_id=1, source_target_pairs={{0,32},{32,0},{4,36},{36,4},{8,40},{40,8},{12,44},{44,12},{16,48},... | collective-permute-start | bytes 6291464 | tf_op jit(solution)/shard_map/ppermute | solution.py:21
  722.1 2.0 copy-start.2
  724.1 90.8 %copy-start.24 = (s32[2,62]{1,0:T(2,128)S(1)}, s32[2,62]{1,0:T(2,128)}, u32[]{:S(2)}) copy-start(s32[2,62]{1,0:T(2,128)} %param.26) | copy-start | bytes 1492
  724.9 367.3 %all-reduce.21.cloned.1.call-start = ((), (), s32[]{:S(2)}) async-start(), calls=%async_computation.6 | async-start | bytes 524288 | tf_op jit(solution)/shard_map/psum | solution.py:26
  762.0 10.3 collective-permute-start.16
  773.4 44.3 %copy-start.20 = (f32[512,128]{1,0:T(8,128)S(1)}, f32[512,128]{1,0:T(8,128)}, u32[]{:S(2)}) copy-start(f32[512,128]{1,0:T(8,128)} %all-reduce.19.cloned.1.call-done) | copy-start | bytes 786436
  773.4 13.4 collective-permute-start.17
  786.9 25.7 %collective-permute-start.18 = (f32[4,512,128]{2,1,0:T(8,128)S(1)}, f32[4,512,128]{2,1,0:T(8,128)S(1)}, u32[]{:S(2)}, u32[]{:S(2)}) collective-permute-start(f32[4,512,128]{2,1,0:T(8,128)S(1)} %maximum_select_fusion.26), channel_id=1, source_target_pairs={{0,16},{16,0},{4,20},{20,4},{8,24},{24,8},{12,28},{28,12},{32,48},... | collective-permute-start | bytes 3145736 | tf_op jit(solution)/shard_map/ppermute | solution.py:21
  814.1 45.5 %collective-permute-start.19 = (f32[8,512,128]{2,1,0:T(8,128)}, f32[8,512,128]{2,1,0:T(8,128)}, u32[]{:S(2)}, u32[]{:S(2)}) collective-permute-start(f32[8,512,128]{2,1,0:T(8,128)} %maximum_select_fusion.12), channel_id=1, source_target_pairs={{0,32},{32,0},{4,36},{36,4},{8,40},{40,8},{12,44},{44,12},{16,48},... | collective-permute-start | bytes 6291464 | tf_op jit(solution)/shard_map/ppermute | solution.py:21
  906.8 91.2 %collective-permute-start.20 = (f32[512,2048]{1,0:T(8,128)}, f32[512,2048]{1,0:T(8,128)}, u32[]{:S(2)}, u32[]{:S(2)}) collective-permute-start(f32[512,2048]{1,0:T(8,128)} %convolution_subtract_fusion.1), channel_id=1, source_target_pairs={{0,64},{64,0},{4,68},{68,4},{8,72},{72,8},{12,76},{76,12},{16,80},... | collective-permute-start | bytes 12582920 | tf_op jit(solution)/shard_map/ppermute | solution.py:21
  1050.8 3.4 copy-start.1
  1055.0 328.3 %all-reduce.23.cloned.1.call-start = ((), (), s32[]{:S(2)}) async-start(), calls=%async_computation.7 | async-start | bytes 524288 | tf_op jit(solution)/shard_map/psum | solution.py:26
  1092.2 10.3 collective-permute-start.21
  1103.5 13.4 collective-permute-start.22
  1117.0 25.3 %collective-permute-start.23 = (f32[4,512,128]{2,1,0:T(8,128)S(1)}, f32[4,512,128]{2,1,0:T(8,128)S(1)}, u32[]{:S(2)}, u32[]{:S(2)}) collective-permute-start(f32[4,512,128]{2,1,0:T(8,128)S(1)} %maximum_select_fusion.28), channel_id=1, source_target_pairs={{0,16},{16,0},{4,20},{20,4},{8,24},{24,8},{12,28},{28,12},{32,48},... | collective-permute-start | bytes 3145736 | tf_op jit(solution)/shard_map/ppermute | solution.py:21
  1142.3 1.1 copy-start.8
  1143.3 45.2 %collective-permute-start.24 = (f32[8,512,128]{2,1,0:T(8,128)S(1)}, f32[8,512,128]{2,1,0:T(8,128)S(1)}, u32[]{:S(2)}, u32[]{:S(2)}) collective-permute-start(f32[8,512,128]{2,1,0:T(8,128)S(1)} %maximum_select_fusion.14), channel_id=1, source_target_pairs={{0,32},{32,0},{4,36},{36,4},{8,40},{40,8},{12,44},{44,12},{16,48},... | collective-permute-start | bytes 6291464 | tf_op jit(solution)/shard_map/ppermute | solution.py:21
  1190.9 91.1 %collective-permute-start.25 = (f32[16,512,128]{2,1,0:T(8,128)}, f32[16,512,128]{2,1,0:T(8,128)}, u32[]{:S(2)}, u32[]{:S(2)}) collective-permute-start(f32[16,512,128]{2,1,0:T(8,128)} %maximum_select_fusion.4), channel_id=1, source_target_pairs={{0,64},{64,0},{4,68},{68,4},{8,72},{72,8},{12,76},{76,12},{16,80},... | collective-permute-start | bytes 12582920 | tf_op jit(solution)/shard_map/ppermute | solution.py:21
  1342.2 3.2 copy-start
  1383.4 10.3 collective-permute-start.26
  1394.7 13.4 collective-permute-start.27
  1408.2 25.3 %collective-permute-start.28 = (f32[4,512,128]{2,1,0:T(8,128)S(1)}, f32[4,512,128]{2,1,0:T(8,128)S(1)}, u32[]{:S(2)}, u32[]{:S(2)}) collective-permute-start(f32[4,512,128]{2,1,0:T(8,128)S(1)} %maximum_select_fusion.30), channel_id=1, source_target_pairs={{0,16},{16,0},{4,20},{20,4},{8,24},{24,8},{12,28},{28,12},{32,48},... | collective-permute-start | bytes 3145736 | tf_op jit(solution)/shard_map/ppermute | solution.py:21
  1433.5 1.0 copy-start.7
  1434.5 49.3 %copy-start.13 = (f32[1,4,128,128]{3,2,1,0:T(8,128)S(1)}, f32[1,4,128,128]{3,2,1,0:T(8,128)}, u32[]{:S(2)}) copy-start(f32[1,4,128,128]{3,2,1,0:T(8,128)} %get-tuple-element.54) | copy-start | bytes 786436
  1434.5 49.3 %copy-start.14 = (f32[1,4,128,128]{3,2,1,0:T(8,128)S(1)}, f32[1,4,128,128]{3,2,1,0:T(8,128)}, u32[]{:S(2)}) copy-start(f32[1,4,128,128]{3,2,1,0:T(8,128)} %get-tuple-element.50) | copy-start | bytes 786436
  1434.5 50.1 %copy-start.15 = (f32[1,4,128,128]{3,2,1,0:T(8,128)S(1)}, f32[1,4,128,128]{3,2,1,0:T(8,128)}, u32[]{:S(2)}) copy-start(f32[1,4,128,128]{3,2,1,0:T(8,128)} %get-tuple-element.46) | copy-start | bytes 786436
  1434.5 50.1 %copy-start.16 = (f32[1,4,128,128]{3,2,1,0:T(8,128)S(1)}, f32[1,4,128,128]{3,2,1,0:T(8,128)}, u32[]{:S(2)}) copy-start(f32[1,4,128,128]{3,2,1,0:T(8,128)} %get-tuple-element.42) | copy-start | bytes 786436
  1434.5 50.9 %copy-start.17 = (f32[1,4,128,128]{3,2,1,0:T(8,128)S(1)}, f32[1,4,128,128]{3,2,1,0:T(8,128)}, u32[]{:S(2)}) copy-start(f32[1,4,128,128]{3,2,1,0:T(8,128)} %get-tuple-element.34) | copy-start | bytes 786436
  1434.5 45.3 %collective-permute-start.29 = (f32[8,512,128]{2,1,0:T(8,128)S(1)}, f32[8,512,128]{2,1,0:T(8,128)S(1)}, u32[]{:S(2)}, u32[]{:S(2)}) collective-permute-start(f32[8,512,128]{2,1,0:T(8,128)S(1)} %maximum_select_fusion.16), channel_id=1, source_target_pairs={{0,32},{32,0},{4,36},{36,4},{8,40},{40,8},{12,44},{44,12},{16,48},... | collective-permute-start | bytes 6291464 | tf_op jit(solution)/shard_map/ppermute | solution.py:21
  1482.2 91.1 %collective-permute-start.30 = (f32[16,512,128]{2,1,0:T(8,128)}, f32[16,512,128]{2,1,0:T(8,128)}, u32[]{:S(2)}, u32[]{:S(2)}) collective-permute-start(f32[16,512,128]{2,1,0:T(8,128)} %maximum_select_fusion.6), channel_id=1, source_target_pairs={{0,64},{64,0},{4,68},{68,4},{8,72},{72,8},{12,76},{76,12},{16,80},... | collective-permute-start | bytes 12582920 | tf_op jit(solution)/shard_map/ppermute | solution.py:21
  1618.2 5.2 copy-start.18
  (1 other events, 0.8 us)
Sparse Core Ops, SparseCore 0:
  11.1 37.3 all-reduce.8
  101.2 37.1 all-reduce.10
  225.6 36.9 all-reduce.12
  346.4 37.1 all-reduce.14
  542.3 36.9 all-reduce.16
  725.0 36.9 all-reduce.18
  1055.1 36.9 all-reduce.20
  1346.3 36.9 all-reduce.22
where the time goes:
time: 1660 us; the launch traced here: 1640 us
  waiting for transfers between devices  982 us (59%)
  other arithmetic  334 us (20%)
  local copies, waits for them, and re-layouts  176 us (11%)
  matrix products  80.3 us (5%)
  starting transfers between devices  55.5 us (3%)
    ppermute x31, waiting for transfers between devices, swapped(): return lax.ppermute(block, axis, route)  687 us
    psum x8, waiting for transfers between devices, broadcast(): return lax.psum(jnp.where(mine, array, jnp.zeros_like(array)), axis)  295 us
    another operation x24, other arithmetic, full_columns(): jnp.linalg.cholesky(blocks[pivot_at % sub_size, pivot_at // sub_size])  99.1 us
    another operation x16, other arithmetic, inverse_lower(): return jax.scipy.linalg.solve_triangular(lower_tri, ident, lower=True)  83.7 us
    select_n x54, other arithmetic, along_cube(): jnp.where(high_half, jnp.concatenate([partner, collected], 0), jnp.concat...  80.5 us
    ppermute x31, starting transfers between devices, swapped(): return lax.ppermute(block, axis, route)  55.2 us
    concatenate x34, local copies, waits for them, and re-layouts, along_cube(): jnp.concatenate([partner, collected], 0)  45.4 us
    dot_general x8, matrix products, eliminate_front(): front_tile = front_tile - jnp.dot(row_terms, col_terms.T, precision=HIGHEST)  43 us
  transfers between devices with their start and end apart: 39, of which 39 were waited for; matrix products, arithmetic and copies ran while one was open for 8% of the time, Pallas kernels for 0%

commit v1 on v0

v1 whole, which is shorter than its diff:
```python
import functools

import jax
import jax.numpy as jnp
from jax import lax
from jax.experimental import pallas as pl
from jax.experimental.pallas import tpu as pltpu
from jax.sharding import PartitionSpec as P

BS = 128
PIVOTS = 2
ROWS = 4
WIDE = PIVOTS * BS
HIGHEST = lax.Precision.HIGHEST
VMEM_LIMIT = 48 * 1024 * 1024


def dot_nn(a, b):
    return jnp.dot(a, b, precision=HIGHEST, preferred_element_type=jnp.float32)


def dot_nt(a, b):
    return lax.dot_general(
        a, b, (((1,), (1,)), ((), ())), precision=HIGHEST, preferred_element_type=jnp.float32
    )


def factor_block(block):
    n = BS
    rows = lax.broadcasted_iota(jnp.int32, (n, n), 0)
    eye = (rows == lax.broadcasted_iota(jnp.int32, (n, n), 1)).astype(jnp.float32)
    parts = [block, eye]
    for j in range(0, n, 2):
        c0 = jnp.broadcast_to(parts[0][:, j : j + 1], (n, n))
        c1 = jnp.broadcast_to(parts[0][:, j + 1 : j + 2], (n, n))
        d0, cross, d1 = c0[j : j + 1], c0[j + 1 : j + 2], c1[j + 1 : j + 2]
        r0 = 1.0 / d0
        ratio = cross * r0
        r1 = 1.0 / (d1 - ratio * cross)
        m0 = jnp.where(rows > j, c0 * r0, 0.0)
        m1 = jnp.where(rows > j + 1, (c1 - m0 * cross) * r1, 0.0)
        done = []
        for part in parts:
            first = part[j : j + 1]
            second = part[j + 1 : j + 2] - ratio * first
            done.append(part - m0 * first - m1 * second)
        parts = done
    diag = jnp.sum(jnp.where(eye > 0, parts[0], 0.0), 1, keepdims=True)
    scale = lax.rsqrt(diag)
    return (parts[0] * scale).T, parts[1] * scale


def pivot_kernel(rows_ref, low_ref, inv_ref):
    c0, i0 = factor_block(rows_ref[:BS, :BS])
    k10 = dot_nt(rows_ref[BS:, :BS], i0)
    c1, i1 = factor_block(rows_ref[BS:, BS:] - dot_nt(k10, k10))
    lane = lax.broadcasted_iota(jnp.int32, (BS, BS), 1)
    sub = lax.broadcasted_iota(jnp.int32, (BS, BS), 0)
    low = lane <= sub
    zero = jnp.zeros((BS, BS), jnp.float32)
    low_ref[:BS, :BS] = jnp.where(low, c0, 0.0)
    low_ref[:BS, BS:] = zero
    low_ref[BS:, :BS] = k10
    low_ref[BS:, BS:] = jnp.where(low, c1, 0.0)
    inv_ref[:BS, :BS] = i0
    inv_ref[:BS, BS:] = zero
    inv_ref[BS:, :BS] = -dot_nn(i1, dot_nn(k10, i0))
    inv_ref[BS:, BS:] = i1


def pivot_factor(pivot_rows):
    shape = jax.ShapeDtypeStruct((WIDE, WIDE), jnp.float32)
    whole = pl.BlockSpec(memory_space=pltpu.VMEM)
    return pl.pallas_call(
        pivot_kernel,
        out_shape=[shape, shape],
        in_specs=[whole],
        out_specs=[whole, whole],
        compiler_params=pltpu.CompilerParams(vmem_limit_bytes=VMEM_LIMIT),
        name="pivot_factor",
    )(pivot_rows)


def update_kernel(cols, has_children, is_root, info_ref, *refs):
    if has_children:
        front_ref, own_ref, other_ref, key_ref, panel_ref, inv_ref, out_ref = refs
    else:
        front_ref, key_ref, panel_ref, inv_ref, out_ref = refs
    at = pl.program_id(0)
    solved = dot_nt(panel_ref[0], inv_ref[...])
    terms = dot_nt(key_ref[...], solved)
    width = ROWS + cols
    for r in range(ROWS):
        span = slice(r * BS, (r + 1) * BS)
        block = front_ref[span, :] - terms[span, :]
        if has_children:
            for which, child_ref in ((0, own_ref), (1, other_ref)):
                source = info_ref[which * width + r]
                present = (source >= 0) & (info_ref[which * width + ROWS + at] >= 0)
                taken = child_ref[pl.ds(jnp.maximum(source, 0) * BS, BS), :]
                block = block + jnp.where(present, taken, 0.0)
        if is_root:
            keep = (info_ref[2 * width + r] >= PIVOTS) & (info_ref[2 * width + ROWS + at] >= PIVOTS)
            block = jnp.where(keep, block, 0.0)
        out_ref[span, :] = block


def update_front(front, own, other, key, panels, inverse, info, panel_of, is_root):
    cols = front.shape[1] // BS
    width = ROWS + cols
    has_children = own is not None
    height = ROWS * BS
    column = pl.BlockSpec((height, BS), lambda c, info: (0, c))
    specs, args = [column], [front]
    if has_children:
        for which, child in ((0, own), (1, other)):
            specs.append(
                pl.BlockSpec(
                    (height, BS),
                    lambda c, info, which=which: (0, jnp.maximum(info[which * width + ROWS + c], 0)),
                )
            )
            args.append(child)
    specs += [
        pl.BlockSpec((height, WIDE), lambda c, info: (0, 0)),
        pl.BlockSpec((1, BS, WIDE), lambda c, info: (panel_of(c), 0, 0)),
        pl.BlockSpec((WIDE, WIDE), lambda c, info: (0, 0)),
    ]
    args += [key, panels, inverse]
    return pl.pallas_call(
        functools.partial(update_kernel, cols, has_children, is_root),
        out_shape=jax.ShapeDtypeStruct(front.shape, jnp.float32),
        grid_spec=pltpu.PrefetchScalarGridSpec(
            num_scalar_prefetch=1, grid=(cols,), in_specs=specs, out_specs=column
        ),
        compiler_params=pltpu.CompilerParams(vmem_limit_bytes=VMEM_LIMIT),
        cost_estimate=pl.CostEstimate(
            flops=2 * height * WIDE * cols * BS * 2,
            bytes_accessed=16 * height * cols * BS,
            transcendentals=0,
        ),
        name="update_front",
    )(info, *args)


def send(block, route):
    pairs = [(a[0] * 4 + a[1], b[0] * 4 + b[1]) for a, b in route]
    return lax.ppermute(block, ("cube", "grid"), pairs)


def both_pivots(piece, cube_count, grid_at):
    got = []
    for step in (1, 2, 3):
        route = [((s, g), (s, g ^ step)) for s in range(cube_count) for g in (0, 1)]
        got.append(send(piece, route))
    near, far, cross = got
    first = jnp.where(grid_at == 0, piece, jnp.where(grid_at == 1, near, jnp.where(grid_at == 2, far, cross)))
    second = jnp.where(grid_at == 1, piece, jnp.where(grid_at == 0, near, jnp.where(grid_at == 3, far, cross)))
    return jnp.concatenate([first, second], -1)


def class_panels(own_rows, sub_size, cube_count, cube_at, grid_at):
    quarter = cube_at % 4
    mine = lax.dynamic_index_in_dim(own_rows, quarter, 0, keepdims=False)
    total = jnp.where(quarter == grid_at, mine, 0.0)
    for step in (1, 2, 3):
        route = [((s, s % 4), (s ^ step, s % 4)) for s in range(cube_count)]
        total = total + send(
            lax.dynamic_index_in_dim(own_rows, quarter ^ step, 0, keepdims=False), route
        )
    groups = None
    if sub_size < cube_count:
        groups = [[b + i for i in range(sub_size)] for b in range(0, cube_count, sub_size)]
    return lax.all_to_all(
        jnp.broadcast_to(total[None], (sub_size, BS, WIDE)), "cube", 0, 0, axis_index_groups=groups
    )


def child_sources(table, child_size, cube_at, grid_at):
    parent_size = 2 * child_size
    slot = cube_at % parent_size
    front = cube_at // child_size
    maps = jnp.stack([table[front], table[front ^ 1]])
    rows = jnp.arange(ROWS) * parent_size + slot
    cols = jnp.arange(parent_size) * 4 + grid_at
    child_ids = jnp.arange(PIVOTS, ROWS * child_size)
    row_hit = maps[:, None, :] == rows[None, :, None]
    col_hit = maps[:, None, :] == cols[None, :, None]
    row_from = jnp.sum(jnp.where(row_hit, child_ids // child_size + 1, 0), 2) - 1
    col_from = jnp.sum(jnp.where(col_hit, child_ids // 4 + 1, 0), 2) - 1
    return jnp.concatenate([row_from, col_from], 1).astype(jnp.int32)


def placed_rows(column, row_from, col_from):
    blocks = column.reshape(ROWS, BS, BS)
    taken = jnp.take(blocks, jnp.maximum(row_from, 0), axis=0)
    keep = (row_from >= 0) & (col_from >= 0)
    return jnp.where(keep[:, None, None], taken, 0.0).reshape(ROWS * BS, BS)


def on_device(
    front_root, front_upper, front_middle, front_lower, place_upper, place_middle, place_lower
):
    cube_count = lax.axis_size("cube")
    cube_at = lax.axis_index("cube")
    grid_at = lax.axis_index("grid")
    stored = (front_root, front_upper, front_middle, front_lower)
    tables = (None, place_upper, place_middle, place_lower)
    factor_list = [None, None, None, None]
    own = other = None
    for depth in (3, 2, 1, 0):
        sub_size = cube_count >> depth
        slot = cube_at % sub_size
        front = stored[depth]
        panel = front[:, :BS]
        row_ids = jnp.arange(ROWS) * sub_size + slot
        col_ids = jnp.arange(sub_size) * 4 + grid_at
        places = jnp.concatenate([row_ids, col_ids]).astype(jnp.int32)
        if own is None:
            info = places
        else:
            half = sub_size // 2
            sources = child_sources(tables[depth + 1], half, cube_at, grid_at)
            first_col = jnp.maximum(sources[:, ROWS], 0)
            mine = lax.dynamic_slice_in_dim(own, first_col[0] * BS, BS, 1)
            info = jnp.concatenate([sources.reshape(-1), places])
            got = send(
                mine,
                [((s, g), (s ^ half, g)) for s in range(cube_count) for g in (0, 1)],
            )
            other = send(own, [((s, g), (s ^ half, g)) for s in range(cube_count) for g in range(4)])
            panel = (
                panel
                + placed_rows(mine, sources[0, :ROWS], sources[0, ROWS])
                + placed_rows(got, sources[1, :ROWS], sources[1, ROWS])
            )
        own_rows = both_pivots(panel, cube_count, grid_at)
        if sub_size == 4:
            pieces = [own_rows]
            for step in (1, 2, 3):
                pieces.append(
                    send(
                        own_rows,
                        [((s, g), (s ^ step, g)) for s in range(cube_count) for g in range(4)],
                    )
                )
            pieces = jnp.stack(pieces)
            panels = lax.dynamic_index_in_dim(pieces, slot ^ grid_at, 0, keepdims=False)
            panels = panels.reshape(ROWS, BS, WIDE)
            pivot_rows = jnp.concatenate(
                [
                    lax.dynamic_index_in_dim(pieces, slot, 0, keepdims=False)[:BS],
                    lax.dynamic_index_in_dim(pieces, slot ^ 1, 0, keepdims=False)[:BS],
                ]
            )
            panel_of = lambda c: c
        else:
            panels = class_panels(
                own_rows.reshape(ROWS, BS, WIDE), sub_size, cube_count, cube_at, grid_at
            )
            pivot_rows = both_pivots(panels[0].reshape(BS, WIDE), cube_count, grid_at)
            pivot_rows = jnp.concatenate([pivot_rows[:, :WIDE], pivot_rows[:, WIDE:]])
            per_row = sub_size // 4
            panel_of = lambda c, per_row=per_row: lax.rem(c, per_row) * 4 + lax.div(c, per_row)
        low, inverse = pivot_factor(pivot_rows)
        solved = dot_nt(own_rows, inverse)
        pivot_slot = jnp.minimum(slot, PIVOTS - 1)
        head = jnp.where(
            slot < PIVOTS, lax.dynamic_slice_in_dim(low, pivot_slot * BS, BS, 0), solved[:BS]
        )
        solved = jnp.concatenate([head, solved[BS:]])
        factor_list[depth] = solved
        own = update_front(
            front, own, other, solved, panels, inverse, info, panel_of, depth == 0
        )
    return (factor_list[0], factor_list[1], factor_list[2], factor_list[3], own)


def solution(mesh):
    return jax.shard_map(
        on_device,
        mesh=mesh,
        in_specs=(
            P("cube", "grid"),
            P("cube", "grid"),
            P("cube", "grid"),
            P("cube", "grid"),
            P(),
            P(),
            P(),
        ),
        out_specs=(
            P("cube", None),
            P("cube", None),
            P("cube", None),
            P("cube", None),
            P("cube", "grid"),
        ),
        check_vma=False,
    )
```

time: 1660 us -> 551 us (0.33)
  waiting for transfers between devices: 982 us -> 279 us
  other arithmetic: 334 us -> 9.41 us
  Pallas kernels: 0 us -> 157 us
  local copies, waits for them, and re-layouts: 176 us -> 19.7 us
  matrix products: 80.3 us -> 3.41 us
    ppermute x31 -> x39, waiting for transfers between devices: 687 us -> 189 us  [send(): return lax.ppermute(block, ('cube', 'grid'), pairs)]
    psum x8 -> x0, waiting for transfers between devices: 295 us -> none  [broadcast(): return lax.psum(jnp.where(mine, array, jnp.zeros_like(array)), axis)]
    another operation x40 -> x5, other arithmetic: 183 us -> 0.3 us  [the longest x2 0.27 us: on_device(): pieces = jnp.stack(pieces)]
    pallas_call x0 -> x8, Pallas kernels: none -> 157 us  [the longest x4 90 us: update_front(): pl.pallas_call(functools.partial(update_kernel, cols, has_children, is_ro...]
    select_n x109 -> x17, other arithmetic: 116 us -> 3.78 us  [the longest x7 3.11 us: both_pivots(): jnp.where(grid_at == 0, piece, jnp.where(grid_at == 1, near, jnp.where(gr...]
    all_to_all x0 -> x3, waiting for transfers between devices: none -> 89.7 us  [class_panels(): lax.all_to_all(jnp.broadcast_to(total[None], (sub_size, BS, WIDE)), 'cube...]
    dot_general x16 -> x4, matrix products: 78 us -> 3.41 us  [dot_nt(): lax.dot_general(a, b, (((1,), (1,)), ((), ())), precision=HIGHEST, prefer...]
    gather x32 -> x6, local copies, waits for them, and re-layouts: 61.4 us -> 3.39 us  [placed_rows(): taken = jnp.take(blocks, jnp.maximum(row_from, 0), axis=0)]
  transfers between devices with their start and end apart: 39 -> 42, of which waited for: 39 -> 25; matrix products, arithmetic and copies ran while one was open for 8% -> 3% of each run, Pallas kernels for 0% -> 9%
where the time goes in v1:
time: 551 us; the launch traced here: 542 us
  waiting for transfers between devices  279 us (51%)
  Pallas kernels  157 us (28%)
  starting transfers between devices  65.2 us (12%)
  local copies, waits for them, and re-layouts  19.7 us (4%)
  other arithmetic  9.41 us (2%)
  between operations  8.18 us (1%)
    ppermute x39, waiting for transfers between devices, send(): return lax.ppermute(block, ('cube', 'grid'), pairs)  189 us
    pallas_call x4, Pallas kernels, update_front(): pl.pallas_call(functools.partial(update_kernel, cols, has_children, is_ro...  90 us
    all_to_all x3, waiting for transfers between devices, class_panels(): lax.all_to_all(jnp.broadcast_to(total[None], (sub_size, BS, WIDE)), 'cube...  89.7 us
    pallas_call x4, Pallas kernels, pivot_factor(): pl.pallas_call(pivot_kernel, out_shape=[shape, shape], in_specs=[whole],...  66.9 us
    ppermute x39, starting transfers between devices, send(): return lax.ppermute(block, ('cube', 'grid'), pairs)  40.8 us
    all_to_all x3, starting transfers between devices, class_panels(): lax.all_to_all(jnp.broadcast_to(total[None], (sub_size, BS, WIDE)), 'cube...  24.4 us
  transfers between devices with their start and end apart: 42, of which 25 were waited for; matrix products, arithmetic and copies ran while one was open for 3% of the time, Pallas kernels for 9%

profile of v1, /device:TPU:30, one launch (start us, length us, event | category | flops | bytes accessed | tf_op | source)
XLA Modules:
  0.0 541.5 jit_solution(1953346549790913658)
XLA Ops:
  1.6 1.3 collective-permute-start.2
  2.9 1.3 collective-permute-start.1
  10.5 1.6 collective-permute-done.2
  12.1 5.6 %collective-permute-done.1 = f32[512,128]{1,0:T(8,128)S(1)} collective-permute-done((f32[512,128]{1,0:T(8,128)S(1)}, f32[512,128]{1,0:T(8,128)S(1)}, u32[]{:S(2)}, u32[]{:S(2)}) %collective-permute-start.1) | collective-permute-done | bytes 262176 | tf_op jit(solution)/shard_map/ppermute | solution.py:148
  18.8 2.0 collective-permute-start.4
  20.8 1.2 collective-permute-start.3
  22.1 1.8 collective-permute-start.5
  24.0 9.0 %collective-permute-done.4 = f32[512,256]{1,0:T(8,128)S(1)} collective-permute-done((f32[512,256]{1,0:T(8,128)S(1)}, f32[512,256]{1,0:T(8,128)S(1)}, u32[]{:S(2)}, u32[]{:S(2)}) %collective-permute-start.4) | collective-permute-done | bytes 524320 | tf_op jit(solution)/shard_map/ppermute | solution.py:148
  33.0 4.1 collective-permute-done.3
  37.1 9.9 %collective-permute-done.5 = f32[512,256]{1,0:T(8,128)S(1)} collective-permute-done((f32[512,256]{1,0:T(8,128)S(1)}, f32[512,256]{1,0:T(8,128)S(1)}, u32[]{:S(2)}, u32[]{:S(2)}) %collective-permute-start.5) | collective-permute-done | bytes 524320 | tf_op jit(solution)/shard_map/ppermute | solution.py:148
  47.3 16.7 %pivot_factor.4 = (f32[256,256]{1,0:T(8,128)S(1)}, f32[256,256]{1,0:T(8,128)S(1)}) custom-call(f32[256,256]{1,0:T(8,128)S(1)} %pad_maximum_fusion.9.rows_ref), custom_call_target="tpu_custom_call" | custom-call | tf_op jit(solution)/shard_map/pivot_factor/pallas_call | solution.py:74
  64.8 6.0 %update_front.4.refs_1_ = f32[512,512]{1,0:T(8,128)S(1)} custom-call(s32[8]{0:T(128)S(1)} %pad_add_fusion.8.info_ref, f32[512,512]{1,0:T(8,128)S(1)} %copy-done.3, f32[512,256]{1,0:T(8,128)S(1)} %pad_maximum_fusion.2.refs_1_, f32[4,128,256]{2,1,0:T(8,128)S(1)} %bitcast.134, f32[256,256]{1,0:T(8,128)S(1)} %get-tuple-element.15.refs_3_), custom_call_target="tpu_custom_call" | custom-call | flops 268435456 | bytes 4194304 | tf_op jit(solution)/shard_map/update_front/pallas_call | solution.py:130
  73.0 1.0 bitcast_add_fusion.4
  74.0 1.3 collective-permute-start.10
  75.3 1.3 collective-permute-start.9
  77.5 9.1 %collective-permute-done.10 = f32[512,128]{1,0:T(8,128)S(1)} collective-permute-done((f32[512,128]{1,0:T(8,128)S(1)}, f32[512,128]{1,0:T(8,128)S(1)}, u32[]{:S(2)}, u32[]{:S(2)}) %collective-permute-start.10) | collective-permute-done | bytes 262176 | tf_op jit(solution)/shard_map/ppermute | solution.py:148
  86.6 8.1 %collective-permute-done.9 = f32[512,128]{1,0:T(8,128)S(1)} collective-permute-done((f32[512,128]{1,0:T(8,128)S(1)}, f32[512,128]{1,0:T(8,128)S(1)}, u32[]{:S(2)}, u32[]{:S(2)}) %collective-permute-start.9) | collective-permute-done | bytes 262176 | tf_op jit(solution)/shard_map/ppermute | solution.py:148
  95.5 1.3 collective-permute-start.13
  98.1 7.0 %collective-permute-done.13 = f32[128,256]{1,0:T(8,128)S(1)} collective-permute-done((f32[128,256]{1,0:T(8,128)S(1)}, f32[128,256]{1,0:T(8,128)S(1)}, u32[]{:S(2)}, u32[]{:S(2)}) %collective-permute-start.13) | collective-permute-done | bytes 131104 | tf_op jit(solution)/shard_map/ppermute | solution.py:148
  105.1 1.1 broadcast_in_dim.158
  106.2 7.8 %all-to-all-start = ((f32[8,128,256]{2,1,0:T(8,128)}), f32[8,128,256]{2,1,0:T(8,128)S(1)}, u32[]{:S(2)}, u32[]{:S(2)}) async-start(f32[8,128,256]{2,1,0:T(8,128)} %broadcast_in_dim.158), calls=%async_computation | async-start | bytes 2097152 | tf_op jit(solution)/shard_map/all_to_all | solution.py:174
  115.5 8.9 %all-to-all-done.refs_4_ = f32[8,128,256]{2,1,0:T(8,128)S(1)} async-done(((f32[8,128,256]{2,1,0:T(8,128)}), f32[8,128,256]{2,1,0:T(8,128)S(1)}, u32[]{:S(2)}, u32[]{:S(2)}) %all-to-all-start) | async-done | bytes 1048608 | tf_op jit(solution)/shard_map/all_to_all | solution.py:174
  124.4 1.3 collective-permute-start.16
  125.7 1.3 collective-permute-start.15
  130.7 2.8 collective-permute-done.15
  133.6 16.7 %pivot_factor.5 = (f32[256,256]{1,0:T(8,128)S(1)}, f32[256,256]{1,0:T(8,128)S(1)}) custom-call(f32[256,256]{1,0:T(8,128)S(1)} %pad_maximum_fusion.10.rows_ref), custom_call_target="tpu_custom_call" | custom-call | tf_op jit(solution)/shard_map/pivot_factor/pallas_call | solution.py:74
  151.1 1.4 copy-done.2
  152.5 12.5 %update_front.5.refs_1_ = f32[512,1024]{1,0:T(8,128)S(1)} custom-call(s32[36]{0:T(128)S(1)} %pad_add_fusion.7.info_ref, f32[512,1024]{1,0:T(8,128)} %refs_0_.5, f32[512,512]{1,0:T(8,128)S(1)} %update_front.4.refs_1_, f32[512,512]{1,0:T(8,128)S(1)} %collective-permute-done.6.refs_2_, f32[512,256]{1,0:T(8,128)S(1)} %pad_maximum_fusion.4.refs_3_, ...), custom_call_target="tpu_custom_call" | custom-call | flops 536870912 | bytes 8388608 | tf_op jit(solution)/shard_map/update_front/pallas_call | solution.py:130
  167.1 1.0 bitcast_add_fusion.2
  168.2 1.3 collective-permute-start.21
  169.5 1.3 collective-permute-start.20
  171.4 18.0 %collective-permute-done.21 = f32[512,128]{1,0:T(8,128)S(1)} collective-permute-done((f32[512,128]{1,0:T(8,128)S(1)}, f32[512,128]{1,0:T(8,128)S(1)}, u32[]{:S(2)}, u32[]{:S(2)}) %collective-permute-start.21) | collective-permute-done | bytes 262176 | tf_op jit(solution)/shard_map/ppermute | solution.py:148
  189.5 7.7 %collective-permute-done.20 = f32[512,128]{1,0:T(8,128)S(1)} collective-permute-done((f32[512,128]{1,0:T(8,128)S(1)}, f32[512,128]{1,0:T(8,128)S(1)}, u32[]{:S(2)}, u32[]{:S(2)}) %collective-permute-start.20) | collective-permute-done | bytes 262176 | tf_op jit(solution)/shard_map/ppermute | solution.py:148
  198.8 1.3 collective-permute-start.24
  200.8 7.3 %collective-permute-done.24 = f32[128,256]{1,0:T(8,128)S(1)} collective-permute-done((f32[128,256]{1,0:T(8,128)S(1)}, f32[128,256]{1,0:T(8,128)S(1)}, u32[]{:S(2)}, u32[]{:S(2)}) %collective-permute-start.24) | collective-permute-done | bytes 131104 | tf_op jit(solution)/shard_map/ppermute | solution.py:148
  208.1 1.5 broadcast_in_dim.161
  209.6 7.4 %all-to-all-start.1 = ((f32[16,128,256]{2,1,0:T(8,128)}), f32[16,128,256]{2,1,0:T(8,128)}, u32[]{:S(2)}, u32[]{:S(2)}) async-start(f32[16,128,256]{2,1,0:T(8,128)} %broadcast_in_dim.161), calls=%async_computation.1 | async-start | bytes 4194304 | tf_op jit(solution)/shard_map/all_to_all | solution.py:174
  219.8 24.3 %all-to-all-done.1.refs_4_ = f32[16,128,256]{2,1,0:T(8,128)} async-done(((f32[16,128,256]{2,1,0:T(8,128)}), f32[16,128,256]{2,1,0:T(8,128)}, u32[]{:S(2)}, u32[]{:S(2)}) %all-to-all-start.1) | async-done | bytes 2097184 | tf_op jit(solution)/shard_map/all_to_all | solution.py:174
  245.0 1.3 collective-permute-start.27
  246.3 1.3 collective-permute-start.26
  249.5 1.7 collective-permute-done.27
  251.3 2.8 collective-permute-done.26
  255.1 16.7 %pivot_factor.6 = (f32[256,256]{1,0:T(8,128)S(1)}, f32[256,256]{1,0:T(8,128)S(1)}) custom-call(f32[256,256]{1,0:T(8,128)S(1)} %pad_maximum_fusion.11.rows_ref), custom_call_target="tpu_custom_call" | custom-call | tf_op jit(solution)/shard_map/pivot_factor/pallas_call | solution.py:74
  271.8 1.6 fusion.16
  273.5 11.3 %collective-permute-done.17.refs_2_ = f32[512,1024]{1,0:T(8,128)} collective-permute-done((f32[512,1024]{1,0:T(8,128)S(1)}, f32[512,1024]{1,0:T(8,128)}, u32[]{:S(2)}, u32[]{:S(2)}) %collective-permute-start.17) | collective-permute-done | bytes 2097184 | tf_op jit(solution)/shard_map/ppermute | solution.py:148
  284.8 24.5 %update_front.6.refs_1_ = f32[512,2048]{1,0:T(8,128)} custom-call(s32[60]{0:T(128)S(1)} %pad_add_fusion.6.info_ref, f32[512,2048]{1,0:T(8,128)} %refs_0_.6, f32[512,1024]{1,0:T(8,128)S(1)} %update_front.5.refs_1_, f32[512,1024]{1,0:T(8,128)} %collective-permute-done.17.refs_2_, f32[512,256]{1,0:T(8,128)S(1)} %pad_maximum_fusion.6.refs_3_, ...), custom_call_target="tpu_custom_call" | custom-call | flops 1073741824 | bytes 16777216 | tf_op jit(solution)/shard_map/update_front/pallas_call | solution.py:130
  312.4 1.0 bitcast_add_fusion
  313.4 1.3 collective-permute-start.31
  314.7 1.3 collective-permute-start.30
  316.7 4.4 collective-permute-done.31
  321.1 9.3 %collective-permute-done.30 = f32[512,128]{1,0:T(8,128)S(1)} collective-permute-done((f32[512,128]{1,0:T(8,128)S(1)}, f32[512,128]{1,0:T(8,128)S(1)}, u32[]{:S(2)}, u32[]{:S(2)}) %collective-permute-start.30) | collective-permute-done | bytes 262176 | tf_op jit(solution)/shard_map/ppermute | solution.py:148
  331.2 1.3 collective-permute-start.34
  333.2 7.3 %collective-permute-done.34 = f32[128,256]{1,0:T(8,128)S(1)} collective-permute-done((f32[128,256]{1,0:T(8,128)S(1)}, f32[128,256]{1,0:T(8,128)S(1)}, u32[]{:S(2)}, u32[]{:S(2)}) %collective-permute-start.34) | collective-permute-done | bytes 131104 | tf_op jit(solution)/shard_map/ppermute | solution.py:148
  340.6 2.5 broadcast_in_dim.163
  343.0 9.2 %all-to-all-start.2 = ((f32[32,128,256]{2,1,0:T(8,128)}), f32[32,128,256]{2,1,0:T(8,128)}, u32[]{:S(2)}, u32[]{:S(2)}) async-start(f32[32,128,256]{2,1,0:T(8,128)} %broadcast_in_dim.163), calls=%async_computation.2 | async-start | bytes 8388608 | tf_op jit(solution)/shard_map/all_to_all | solution.py:174
  352.2 1.5 collective-permute-start.38
  353.7 56.6 %all-to-all-done.2.refs_4_ = f32[32,128,256]{2,1,0:T(8,128)} async-done(((f32[32,128,256]{2,1,0:T(8,128)}), f32[32,128,256]{2,1,0:T(8,128)}, u32[]{:S(2)}, u32[]{:S(2)}) %all-to-all-start.2) | async-done | bytes 4194336 | tf_op jit(solution)/shard_map/all_to_all | solution.py:174
  411.2 1.3 collective-permute-start.37
  412.5 1.3 collective-permute-start.36
  414.7 2.8 collective-permute-done.37
  417.5 2.8 collective-permute-done.36
  421.3 16.7 %pivot_factor.7 = (f32[256,256]{1,0:T(8,128)S(1)}, f32[256,256]{1,0:T(8,128)S(1)}) custom-call(f32[256,256]{1,0:T(8,128)S(1)} %pad_maximum_fusion.12.rows_ref), custom_call_target="tpu_custom_call" | custom-call | tf_op jit(solution)/shard_map/pivot_factor/pallas_call | solution.py:74
  438.8 55.4 %collective-permute-done.38.refs_2_ = f32[512,2048]{1,0:T(8,128)} collective-permute-done((f32[512,2048]{1,0:T(8,128)}, f32[512,2048]{1,0:T(8,128)}, u32[]{:S(2)}, u32[]{:S(2)}) %collective-permute-start.38) | collective-permute-done | bytes 4194336 | tf_op jit(solution)/shard_map/ppermute | solution.py:148
  494.2 46.9 %update_front.7 = f32[512,4096]{1,0:T(8,128)} custom-call(s32[108]{0:T(128)S(1)} %pad_add_fusion.9.info_ref, f32[512,4096]{1,0:T(8,128)} %refs_0_.7, f32[512,2048]{1,0:T(8,128)S(1)} %copy-done, f32[512,2048]{1,0:T(8,128)} %collective-permute-done.38.refs_2_, f32[512,256]{1,0:T(8,128)S(1)} %pad_maximum_fusion.8.refs_3_, ...), custom_call_target="tpu_custom_call" | custom-call | flops 2147483648 | bytes 33554432 | tf_op jit(solution)/shard_map/update_front/pallas_call | solution.py:130
  (173 shorter events, 34.6 us)
Async XLA Ops:
  1.6 10.5 %collective-permute-start.2 = (f32[512,128]{1,0:T(8,128)S(1)}, f32[512,128]{1,0:T(8,128)S(1)}, u32[]{:S(2)}, u32[]{:S(2)}) collective-permute-start(f32[512,128]{1,0:T(8,128)S(1)} %slice.117), channel_id=1, source_target_pairs={{0,3},{1,2},{4,7},{5,6},{8,11},{9,10},{12,15},{13,14},{16,19},{17,... | collective-permute-start | bytes 786440 | tf_op jit(solution)/shard_map/ppermute | solution.py:148
  2.9 14.8 %collective-permute-start.1 = (f32[512,128]{1,0:T(8,128)S(1)}, f32[512,128]{1,0:T(8,128)S(1)}, u32[]{:S(2)}, u32[]{:S(2)}) collective-permute-start(f32[512,128]{1,0:T(8,128)S(1)} %slice.117), channel_id=1, source_target_pairs={{0,2},{1,3},{4,6},{5,7},{8,10},{9,11},{12,14},{13,15},{16,18},{17,... | collective-permute-start | bytes 786440 | tf_op jit(solution)/shard_map/ppermute | solution.py:148
  4.2 13.5 %collective-permute-start = (f32[512,128]{1,0:T(8,128)S(1)}, f32[512,128]{1,0:T(8,128)S(1)}, u32[]{:S(2)}, u32[]{:S(2)}) collective-permute-start(f32[512,128]{1,0:T(8,128)S(1)} %slice.117), channel_id=1, source_target_pairs={{0,1},{1,0},{4,5},{5,4},{8,9},{9,8},{12,13},{13,12},{16,17},{17,16... | collective-permute-start | bytes 786440 | tf_op jit(solution)/shard_map/ppermute | solution.py:148
  18.8 14.2 %collective-permute-start.4 = (f32[512,256]{1,0:T(8,128)S(1)}, f32[512,256]{1,0:T(8,128)S(1)}, u32[]{:S(2)}, u32[]{:S(2)}) collective-permute-start(f32[512,256]{1,0:T(8,128)S(1)} %get-tuple-element.60), channel_id=1, source_target_pairs={{0,8},{1,9},{2,10},{3,11},{4,12},{5,13},{6,14},{7,15},{8,0},{9,1},... | collective-permute-start | bytes 1572872 | tf_op jit(solution)/shard_map/ppermute | solution.py:148
  20.8 16.3 %collective-permute-start.3 = (f32[512,256]{1,0:T(8,128)S(1)}, f32[512,256]{1,0:T(8,128)S(1)}, u32[]{:S(2)}, u32[]{:S(2)}) collective-permute-start(f32[512,256]{1,0:T(8,128)S(1)} %get-tuple-element.60), channel_id=1, source_target_pairs={{0,4},{1,5},{2,6},{3,7},{4,0},{5,1},{6,2},{7,3},{8,12},{9,13},{10,... | collective-permute-start | bytes 1572872 | tf_op jit(solution)/shard_map/ppermute | solution.py:148
  22.1 25.0 %collective-permute-start.5 = (f32[512,256]{1,0:T(8,128)S(1)}, f32[512,256]{1,0:T(8,128)S(1)}, u32[]{:S(2)}, u32[]{:S(2)}) collective-permute-start(f32[512,256]{1,0:T(8,128)S(1)} %get-tuple-element.60), channel_id=1, source_target_pairs={{0,12},{1,13},{2,14},{3,15},{4,8},{5,9},{6,10},{7,11},{8,4},{9,5},... | collective-permute-start | bytes 1572872 | tf_op jit(solution)/shard_map/ppermute | solution.py:148
  47.3 17.5 %copy-start.3 = (f32[512,512]{1,0:T(8,128)S(1)}, f32[512,512]{1,0:T(8,128)}, u32[]{:S(2)}) copy-start(f32[512,512]{1,0:T(8,128)} %refs_0_.4) | copy-start | bytes 3145732
  64.8 6.0 %copy-start.7 = (f32[512,256]{1,0:T(8,128)}, f32[512,256]{1,0:T(8,128)S(1)}, u32[]{:S(2)}) copy-start(f32[512,256]{1,0:T(8,128)S(1)} %pad_maximum_fusion.2.refs_1_) | copy-start | bytes 1572868
  64.8 6.8 %copy-start.9 = (s32[2,62]{1,0:T(2,128)S(1)}, s32[2,62]{1,0:T(2,128)}, u32[]{:S(2)}) copy-start(s32[2,62]{1,0:T(2,128)} %param.13) | copy-start | bytes 1492
  70.9 1.4 collective-permute-start.7
  74.0 12.6 %collective-permute-start.10 = (f32[512,128]{1,0:T(8,128)S(1)}, f32[512,128]{1,0:T(8,128)S(1)}, u32[]{:S(2)}, u32[]{:S(2)}) collective-permute-start(f32[512,128]{1,0:T(8,128)S(1)} %bitcast_add_fusion.4), channel_id=1, source_target_pairs={{0,3},{1,2},{4,7},{5,6},{8,11},{9,10},{12,15},{13,14},{16,19},{17,... | collective-permute-start | bytes 786440 | tf_op jit(solution)/shard_map/ppermute | solution.py:148
  75.3 19.4 %collective-permute-start.9 = (f32[512,128]{1,0:T(8,128)S(1)}, f32[512,128]{1,0:T(8,128)S(1)}, u32[]{:S(2)}, u32[]{:S(2)}) collective-permute-start(f32[512,128]{1,0:T(8,128)S(1)} %bitcast_add_fusion.4), channel_id=1, source_target_pairs={{0,2},{1,3},{4,6},{5,7},{8,10},{9,11},{12,14},{13,15},{16,18},{17,... | collective-permute-start | bytes 786440 | tf_op jit(solution)/shard_map/ppermute | solution.py:148
  76.6 18.1 %collective-permute-start.8 = (f32[512,128]{1,0:T(8,128)S(1)}, f32[512,128]{1,0:T(8,128)S(1)}, u32[]{:S(2)}, u32[]{:S(2)}) collective-permute-start(f32[512,128]{1,0:T(8,128)S(1)} %bitcast_add_fusion.4), channel_id=1, source_target_pairs={{0,1},{1,0},{4,5},{5,4},{8,9},{9,8},{12,13},{13,12},{16,17},{17,16... | collective-permute-start | bytes 786440 | tf_op jit(solution)/shard_map/ppermute | solution.py:148
  94.9 3.2 collective-permute-start.11
  95.5 9.5 %collective-permute-start.13 = (f32[128,256]{1,0:T(8,128)S(1)}, f32[128,256]{1,0:T(8,128)S(1)}, u32[]{:S(2)}, u32[]{:S(2)}) collective-permute-start(f32[128,256]{1,0:T(8,128)S(1)} %get-tuple-element.57), channel_id=1, source_target_pairs={{0,12},{5,9},{10,6},{15,3},{16,28},{21,25},{26,22},{31,19},{32,44}... | collective-permute-start | bytes 393224 | tf_op jit(solution)/shard_map/ppermute | solution.py:148
  96.8 8.2 %collective-permute-start.12 = (f32[128,256]{1,0:T(8,128)S(1)}, f32[128,256]{1,0:T(8,128)S(1)}, u32[]{:S(2)}, u32[]{:S(2)}) collective-permute-start(f32[128,256]{1,0:T(8,128)S(1)} %get-tuple-element.58), channel_id=1, source_target_pairs={{0,8},{5,13},{10,2},{15,7},{16,24},{21,29},{26,18},{31,23},{32,40}... | collective-permute-start | bytes 393224 | tf_op jit(solution)/shard_map/ppermute | solution.py:148
  106.2 18.2 %all-to-all-start = ((f32[8,128,256]{2,1,0:T(8,128)}), f32[8,128,256]{2,1,0:T(8,128)S(1)}, u32[]{:S(2)}, u32[]{:S(2)}) async-start(f32[8,128,256]{2,1,0:T(8,128)} %broadcast_in_dim.158), calls=%async_computation | async-start | bytes 2097152 | tf_op jit(solution)/shard_map/all_to_all | solution.py:174
  124.4 26.6 %copy-start.1 = (f32[8,128,256]{2,1,0:T(8,128)}, f32[8,128,256]{2,1,0:T(8,128)S(1)}, u32[]{:S(2)}) copy-start(f32[8,128,256]{2,1,0:T(8,128)S(1)} %all-to-all-done.refs_4_) | copy-start | bytes 3145732
  124.4 6.3 %collective-permute-start.16 = (f32[128,256]{1,0:T(8,128)S(1)}, f32[128,256]{1,0:T(8,128)S(1)}, u32[]{:S(2)}, u32[]{:S(2)}) collective-permute-start(f32[128,256]{1,0:T(8,128)S(1)} %slice_bitcast_fusion.2), channel_id=1, source_target_pairs={{0,3},{1,2},{4,7},{5,6},{8,11},{9,10},{12,15},{13,14},{16,19},{17,... | collective-permute-start | bytes 393224 | tf_op jit(solution)/shard_map/ppermute | solution.py:148
  125.7 7.8 %collective-permute-start.15 = (f32[128,256]{1,0:T(8,128)S(1)}, f32[128,256]{1,0:T(8,128)S(1)}, u32[]{:S(2)}, u32[]{:S(2)}) collective-permute-start(f32[128,256]{1,0:T(8,128)S(1)} %slice_bitcast_fusion.2), channel_id=1, source_target_pairs={{0,2},{1,3},{4,6},{5,7},{8,10},{9,11},{12,14},{13,15},{16,18},{17,... | collective-permute-start | bytes 393224 | tf_op jit(solution)/shard_map/ppermute | solution.py:148
  127.0 6.5 %collective-permute-start.14 = (f32[128,256]{1,0:T(8,128)S(1)}, f32[128,256]{1,0:T(8,128)S(1)}, u32[]{:S(2)}, u32[]{:S(2)}) collective-permute-start(f32[128,256]{1,0:T(8,128)S(1)} %slice_bitcast_fusion.2), channel_id=1, source_target_pairs={{0,1},{1,0},{4,5},{5,4},{8,9},{9,8},{12,13},{13,12},{16,17},{17,16... | collective-permute-start | bytes 393224 | tf_op jit(solution)/shard_map/ppermute | solution.py:148
  129.0 22.0 %collective-permute-start.6 = (f32[512,512]{1,0:T(8,128)S(1)}, f32[512,512]{1,0:T(8,128)S(1)}, u32[]{:S(2)}, u32[]{:S(2)}) collective-permute-start(f32[512,512]{1,0:T(8,128)S(1)} %update_front.4.refs_1_), channel_id=1, source_target_pairs={{0,16},{1,17},{2,18},{3,19},{4,20},{5,21},{6,22},{7,23},{8,24},{9,... | collective-permute-start | bytes 3145736 | tf_op jit(solution)/shard_map/ppermute | solution.py:148
  151.1 14.0 %copy-start.5 = (f32[512,256]{1,0:T(8,128)}, f32[512,256]{1,0:T(8,128)S(1)}, u32[]{:S(2)}) copy-start(f32[512,256]{1,0:T(8,128)S(1)} %pad_maximum_fusion.4.refs_3_) | copy-start | bytes 1572868
  151.1 1.4 copy-start.2
  165.1 1.4 collective-permute-start.18
  168.2 21.3 %collective-permute-start.21 = (f32[512,128]{1,0:T(8,128)S(1)}, f32[512,128]{1,0:T(8,128)S(1)}, u32[]{:S(2)}, u32[]{:S(2)}) collective-permute-start(f32[512,128]{1,0:T(8,128)S(1)} %bitcast_add_fusion.2), channel_id=1, source_target_pairs={{0,3},{1,2},{4,7},{5,6},{8,11},{9,10},{12,15},{13,14},{16,19},{17,... | collective-permute-start | bytes 786440 | tf_op jit(solution)/shard_map/ppermute | solution.py:148
  169.5 27.7 %collective-permute-start.20 = (f32[512,128]{1,0:T(8,128)S(1)}, f32[512,128]{1,0:T(8,128)S(1)}, u32[]{:S(2)}, u32[]{:S(2)}) collective-permute-start(f32[512,128]{1,0:T(8,128)S(1)} %bitcast_add_fusion.2), channel_id=1, source_target_pairs={{0,2},{1,3},{4,6},{5,7},{8,10},{9,11},{12,14},{13,15},{16,18},{17,... | collective-permute-start | bytes 786440 | tf_op jit(solution)/shard_map/ppermute | solution.py:148
  170.8 26.4 %collective-permute-start.19 = (f32[512,128]{1,0:T(8,128)S(1)}, f32[512,128]{1,0:T(8,128)S(1)}, u32[]{:S(2)}, u32[]{:S(2)}) collective-permute-start(f32[512,128]{1,0:T(8,128)S(1)} %bitcast_add_fusion.2), channel_id=1, source_target_pairs={{0,1},{1,0},{4,5},{5,4},{8,9},{9,8},{12,13},{13,12},{16,17},{17,16... | collective-permute-start | bytes 786440 | tf_op jit(solution)/shard_map/ppermute | solution.py:148
  197.3 0.7 copy-start.8
  198.1 2.7 collective-permute-start.22
  198.8 9.3 %collective-permute-start.24 = (f32[128,256]{1,0:T(8,128)S(1)}, f32[128,256]{1,0:T(8,128)S(1)}, u32[]{:S(2)}, u32[]{:S(2)}) collective-permute-start(f32[128,256]{1,0:T(8,128)S(1)} %get-tuple-element.54), channel_id=1, source_target_pairs={{0,12},{5,9},{10,6},{15,3},{16,28},{21,25},{26,22},{31,19},{32,44}... | collective-permute-start | bytes 393224 | tf_op jit(solution)/shard_map/ppermute | solution.py:148
  200.1 8.0 %collective-permute-start.23 = (f32[128,256]{1,0:T(8,128)S(1)}, f32[128,256]{1,0:T(8,128)S(1)}, u32[]{:S(2)}, u32[]{:S(2)}) collective-permute-start(f32[128,256]{1,0:T(8,128)S(1)} %get-tuple-element.55), channel_id=1, source_target_pairs={{0,8},{5,13},{10,2},{15,7},{16,24},{21,29},{26,18},{31,23},{32,40}... | collective-permute-start | bytes 393224 | tf_op jit(solution)/shard_map/ppermute | solution.py:148
  209.6 34.5 %all-to-all-start.1 = ((f32[16,128,256]{2,1,0:T(8,128)}), f32[16,128,256]{2,1,0:T(8,128)}, u32[]{:S(2)}, u32[]{:S(2)}) async-start(f32[16,128,256]{2,1,0:T(8,128)} %broadcast_in_dim.161), calls=%async_computation.1 | async-start | bytes 4194304 | tf_op jit(solution)/shard_map/all_to_all | solution.py:174
  217.7 67.1 %collective-permute-start.17 = (f32[512,1024]{1,0:T(8,128)S(1)}, f32[512,1024]{1,0:T(8,128)}, u32[]{:S(2)}, u32[]{:S(2)}) collective-permute-start(f32[512,1024]{1,0:T(8,128)S(1)} %update_front.5.refs_1_), channel_id=1, source_target_pairs={{0,32},{1,33},{2,34},{3,35},{4,36},{5,37},{6,38},{7,39},{8,40},{9,... | collective-permute-start | bytes 6291464 | tf_op jit(solution)/shard_map/ppermute | solution.py:148
  245.0 6.3 %collective-permute-start.27 = (f32[128,256]{1,0:T(8,128)S(1)}, f32[128,256]{1,0:T(8,128)S(1)}, u32[]{:S(2)}, u32[]{:S(2)}) collective-permute-start(f32[128,256]{1,0:T(8,128)S(1)} %slice_bitcast_fusion.1), channel_id=1, source_target_pairs={{0,3},{1,2},{4,7},{5,6},{8,11},{9,10},{12,15},{13,14},{16,19},{17,... | collective-permute-start | bytes 393224 | tf_op jit(solution)/shard_map/ppermute | solution.py:148
  246.3 7.8 %collective-permute-start.26 = (f32[128,256]{1,0:T(8,128)S(1)}, f32[128,256]{1,0:T(8,128)S(1)}, u32[]{:S(2)}, u32[]{:S(2)}) collective-permute-start(f32[128,256]{1,0:T(8,128)S(1)} %slice_bitcast_fusion.1), channel_id=1, source_target_pairs={{0,2},{1,3},{4,6},{5,7},{8,10},{9,11},{12,14},{13,15},{16,18},{17,... | collective-permute-start | bytes 393224 | tf_op jit(solution)/shard_map/ppermute | solution.py:148
  247.6 6.5 %collective-permute-start.25 = (f32[128,256]{1,0:T(8,128)S(1)}, f32[128,256]{1,0:T(8,128)S(1)}, u32[]{:S(2)}, u32[]{:S(2)}) collective-permute-start(f32[128,256]{1,0:T(8,128)S(1)} %slice_bitcast_fusion.1), channel_id=1, source_target_pairs={{0,1},{1,0},{4,5},{5,4},{8,9},{9,8},{12,13},{13,12},{16,17},{17,16... | collective-permute-start | bytes 393224 | tf_op jit(solution)/shard_map/ppermute | solution.py:148
  273.5 35.9 %copy-start.6 = (f32[512,256]{1,0:T(8,128)}, f32[512,256]{1,0:T(8,128)S(1)}, u32[]{:S(2)}) copy-start(f32[512,256]{1,0:T(8,128)S(1)} %pad_maximum_fusion.6.refs_3_) | copy-start | bytes 1572868
  310.4 1.4 collective-permute-start.28
  313.4 7.7 %collective-permute-start.31 = (f32[512,128]{1,0:T(8,128)S(1)}, f32[512,128]{1,0:T(8,128)S(1)}, u32[]{:S(2)}, u32[]{:S(2)}) collective-permute-start(f32[512,128]{1,0:T(8,128)S(1)} %bitcast_add_fusion), channel_id=1, source_target_pairs={{0,3},{1,2},{4,7},{5,6},{8,11},{9,10},{12,15},{13,14},{16,19},{17,... | collective-permute-start | bytes 786440 | tf_op jit(solution)/shard_map/ppermute | solution.py:148
  314.7 15.7 %collective-permute-start.30 = (f32[512,128]{1,0:T(8,128)S(1)}, f32[512,128]{1,0:T(8,128)S(1)}, u32[]{:S(2)}, u32[]{:S(2)}) collective-permute-start(f32[512,128]{1,0:T(8,128)S(1)} %bitcast_add_fusion), channel_id=1, source_target_pairs={{0,2},{1,3},{4,6},{5,7},{8,10},{9,11},{12,14},{13,15},{16,18},{17,... | collective-permute-start | bytes 786440 | tf_op jit(solution)/shard_map/ppermute | solution.py:148
  316.0 14.4 %collective-permute-start.29 = (f32[512,128]{1,0:T(8,128)S(1)}, f32[512,128]{1,0:T(8,128)S(1)}, u32[]{:S(2)}, u32[]{:S(2)}) collective-permute-start(f32[512,128]{1,0:T(8,128)S(1)} %bitcast_add_fusion), channel_id=1, source_target_pairs={{0,1},{1,0},{4,5},{5,4},{8,9},{9,8},{12,13},{13,12},{16,17},{17,16... | collective-permute-start | bytes 786440 | tf_op jit(solution)/shard_map/ppermute | solution.py:148
  330.6 2.7 collective-permute-start.32
  331.2 9.3 %collective-permute-start.34 = (f32[128,256]{1,0:T(8,128)S(1)}, f32[128,256]{1,0:T(8,128)S(1)}, u32[]{:S(2)}, u32[]{:S(2)}) collective-permute-start(f32[128,256]{1,0:T(8,128)S(1)} %get-tuple-element.51), channel_id=1, source_target_pairs={{0,12},{5,9},{10,6},{15,3},{16,28},{21,25},{26,22},{31,19},{32,44}... | collective-permute-start | bytes 393224 | tf_op jit(solution)/shard_map/ppermute | solution.py:148
  332.5 8.0 %collective-permute-start.33 = (f32[128,256]{1,0:T(8,128)S(1)}, f32[128,256]{1,0:T(8,128)S(1)}, u32[]{:S(2)}, u32[]{:S(2)}) collective-permute-start(f32[128,256]{1,0:T(8,128)S(1)} %get-tuple-element.52), channel_id=1, source_target_pairs={{0,8},{5,13},{10,2},{15,7},{16,24},{21,29},{26,18},{31,23},{32,40}... | collective-permute-start | bytes 393224 | tf_op jit(solution)/shard_map/ppermute | solution.py:148
  343.0 67.3 %all-to-all-start.2 = ((f32[32,128,256]{2,1,0:T(8,128)}), f32[32,128,256]{2,1,0:T(8,128)}, u32[]{:S(2)}, u32[]{:S(2)}) async-start(f32[32,128,256]{2,1,0:T(8,128)} %broadcast_in_dim.163), calls=%async_computation.2 | async-start | bytes 8388608 | tf_op jit(solution)/shard_map/all_to_all | solution.py:174
  352.2 141.9 %collective-permute-start.38 = (f32[512,2048]{1,0:T(8,128)}, f32[512,2048]{1,0:T(8,128)}, u32[]{:S(2)}, u32[]{:S(2)}) collective-permute-start(f32[512,2048]{1,0:T(8,128)} %update_front.6.refs_1_), channel_id=1, source_target_pairs={{0,64},{1,65},{2,66},{3,67},{4,68},{5,69},{6,70},{7,71},{8,72},{9,... | collective-permute-start | bytes 12582920 | tf_op jit(solution)/shard_map/ppermute | solution.py:148
  411.2 6.3 %collective-permute-start.37 = (f32[128,256]{1,0:T(8,128)S(1)}, f32[128,256]{1,0:T(8,128)S(1)}, u32[]{:S(2)}, u32[]{:S(2)}) collective-permute-start(f32[128,256]{1,0:T(8,128)S(1)} %slice_bitcast_fusion), channel_id=1, source_target_pairs={{0,3},{1,2},{4,7},{5,6},{8,11},{9,10},{12,15},{13,14},{16,19},{17,... | collective-permute-start | bytes 393224 | tf_op jit(solution)/shard_map/ppermute | solution.py:148
  412.5 7.8 %collective-permute-start.36 = (f32[128,256]{1,0:T(8,128)S(1)}, f32[128,256]{1,0:T(8,128)S(1)}, u32[]{:S(2)}, u32[]{:S(2)}) collective-permute-start(f32[128,256]{1,0:T(8,128)S(1)} %slice_bitcast_fusion), channel_id=1, source_target_pairs={{0,2},{1,3},{4,6},{5,7},{8,10},{9,11},{12,14},{13,15},{16,18},{17,... | collective-permute-start | bytes 393224 | tf_op jit(solution)/shard_map/ppermute | solution.py:148
  413.8 6.5 %collective-permute-start.35 = (f32[128,256]{1,0:T(8,128)S(1)}, f32[128,256]{1,0:T(8,128)S(1)}, u32[]{:S(2)}, u32[]{:S(2)}) collective-permute-start(f32[128,256]{1,0:T(8,128)S(1)} %slice_bitcast_fusion), channel_id=1, source_target_pairs={{0,1},{1,0},{4,5},{5,4},{8,9},{9,8},{12,13},{13,12},{16,17},{17,16... | collective-permute-start | bytes 393224 | tf_op jit(solution)/shard_map/ppermute | solution.py:148
  421.3 72.9 %copy-start = (f32[512,2048]{1,0:T(8,128)S(1)}, f32[512,2048]{1,0:T(8,128)}, u32[]{:S(2)}) copy-start(f32[512,2048]{1,0:T(8,128)} %update_front.6.refs_1_) | copy-start | bytes 12582916
  438.8 102.3 %copy-start.4 = (f32[512,256]{1,0:T(8,128)}, f32[512,256]{1,0:T(8,128)S(1)}, u32[]{:S(2)}) copy-start(f32[512,256]{1,0:T(8,128)S(1)} %pad_maximum_fusion.8.refs_3_) | copy-start | bytes 1572868
